TPU v7x, 1024 devices: a whole 8x8x8 slice. The times are simulated.
1024 devices in a mesh: row: 64 (over x, z), col: 16 (over y, core).
Axes of the slice: x: 8, y: 8, z: 8, core: 2. Of those that a mesh axis runs over, the one named last changes fastest.
Arguments:
- pooled: bfloat16 [4096, 64, 1024], P(('row', 'col'))
- upstream: bfloat16 [4096, 64, 1024], P(('row', 'col')), may hold values from -6 to 6
- cross_weight: bfloat16 [1024, 1024], replicated, may hold values from -0.1875 to 0.1875
- cross_bias: float32 [1024], replicated, may hold values from -3 to 3
- deep_weight: bfloat16 [1024, 1024], replicated, may hold values from -0.1875 to 0.1875
- deep_bias: float32 [1024], replicated, may hold values from -3 to 3
- bag_entries: int32 [4096, 64, 2], P('row'), may hold values from 0 to 4095
- touched_rows: int32 [4096], P('row'), may hold values from 0 to 1023, as said below
- table: float32 [65536, 1024], P('row', 'col'), may hold values from -4 to 4
- first_moment: float32 [65536, 1024], P('row', 'col'), may hold values from -6 to 6
- second_moment: float32 [65536], P('row'), may hold values from 0.002 to 0.2
- step_counts: int32 [65536], P('row'), may hold values from 0 to 7
Outputs:
- new_table: float32 [65536, 1024], P('row', 'col')
- new_first: float32 [65536, 1024], P('row', 'col')
- new_second: float32 [65536], P('row')
Inputs may be any that keep to these rules, and one draw needn't show every extreme that they name: `bag_entries`: entry e stands for row touched_rows[e] of table row shard e // 64. `touched_rows`: within each block of 64 entries (one row shard's) the rows are distinct.
All inputs are finite; a program needn't handle non-finite values.
Results may differ from a plain program's by a relative error of at most 0.00075.
The roundings to bfloat16 on the way count: a program that leaves them out, or rounds other values in their place, can miss the bound.
Values may be sent and summed in bfloat16 or wider, within the bound.
A program may use at most 32 MiB of HBM per device.

v0:
```python
import jax
import jax.numpy as jnp
from jax import lax
from jax.sharding import PartitionSpec as P


def cross_back(inputs, upstream, cross_weight, cross_bias, deep_weight, deep_bias):
    wide_in = inputs.astype(jnp.float32)
    scaled = jnp.dot(inputs, cross_weight, preferred_element_type=jnp.float32) + cross_bias
    crossed = (wide_in * scaled + wide_in).astype(jnp.bfloat16)
    hidden = jnp.dot(crossed, deep_weight, preferred_element_type=jnp.float32) + deep_bias
    sigmoid_h = jax.nn.sigmoid(hidden)
    hidden_grad = (
        upstream.astype(jnp.float32) * sigmoid_h * (1.0 + hidden * (1.0 - sigmoid_h))
    ).astype(jnp.bfloat16)
    crossed_grad = lax.dot_general(
        hidden_grad, deep_weight, (((1,), (1,)), ((), ())), preferred_element_type=jnp.float32
    )
    product = (crossed_grad * wide_in).astype(jnp.bfloat16)
    back_term = lax.dot_general(
        product, cross_weight, (((1,), (1,)), ((), ())), preferred_element_type=jnp.float32
    )
    return (crossed_grad * scaled + back_term + crossed_grad).astype(jnp.bfloat16)


def adam_rows(weights, first, second, steps, grads, mean_square):
    first_new = 0.9 * first + 0.1 * grads
    second_new = 0.999 * second + 0.001 * mean_square
    step_float = (steps + 1).astype(jnp.float32)
    first_hat = first_new / (1.0 - jnp.power(0.9, step_float))[:, None]
    second_hat = second_new / (1.0 - jnp.power(0.999, step_float))
    weights_new = weights - 0.01 * first_hat / (jnp.sqrt(second_hat)[:, None] + 1e-08)
    return (weights_new, first_new, second_new)


def body(
    pooled,
    upstream,
    cross_weight,
    cross_bias,
    deep_weight,
    deep_bias,
    bag_entries,
    touched_rows,
    table,
    first_moment,
    second_moment,
    step_counts,
):
    samples, fields, feat_width = pooled.shape
    token_rows = samples * fields
    grad_tokens = cross_back(
        pooled.reshape(token_rows, feat_width),
        upstream.reshape(token_rows, upstream.shape[2]),
        cross_weight,
        cross_bias,
        deep_weight,
        deep_bias,
    )
    pooled_grad = grad_tokens.reshape(samples, fields, feat_width)
    regrouped = lax.all_to_all(pooled_grad, "col", split_axis=2, concat_axis=0, tiled=True)
    slice_width = regrouped.shape[2]
    occurrences = regrouped.reshape(-1, slice_width).astype(jnp.float32)
    entry_ids = bag_entries.reshape(occurrences.shape[0], bag_entries.shape[2])
    touched = touched_rows.shape[0]
    owners = lax.axis_size("row")
    all_entries = owners * touched
    all_terms = jnp.zeros((all_entries, slice_width), jnp.float32)
    for bag_pos in range(entry_ids.shape[1]):
        all_terms = all_terms + jax.ops.segment_sum(
            occurrences, entry_ids[:, bag_pos], num_segments=all_entries
        )
    entry_grads = lax.psum_scatter(all_terms, "row", scatter_dimension=0, tiled=True)
    square_sums = lax.psum(jnp.sum(entry_grads * entry_grads, axis=1), "col")
    mean_square = square_sums / (slice_width * lax.axis_size("col"))
    weights_new, first_new, second_new = adam_rows(
        table[touched_rows],
        first_moment[touched_rows],
        second_moment[touched_rows],
        step_counts[touched_rows],
        entry_grads,
        mean_square,
    )
    new_table = table.at[touched_rows].set(weights_new)
    new_first = first_moment.at[touched_rows].set(first_new)
    new_second = second_moment.at[touched_rows].set(second_new)
    return (new_table, new_first, new_second)


def solution(mesh):
    in_specs = (
        P(("row", "col"), None, None),
        P(("row", "col"), None, None),
        P(),
        P(),
        P(),
        P(),
        P("row", None, None),
        P("row"),
        P("row", "col"),
        P("row", "col"),
        P("row"),
        P("row"),
    )
    out_specs = (P("row", "col"), P("row", "col"), P("row"))
    return jax.shard_map(body, mesh=mesh, in_specs=in_specs, out_specs=out_specs, check_vma=False)
```

profile of v0, /device:TPU:1, one launch (start us, length us, event | category | flops | bytes accessed | tf_op | source)
XLA Modules:
  0.0 399.9 jit_solution(4504838880819686108)
XLA Ops:
  7.2 0.8 copy.39
  8.0 0.8 copy-done
  8.8 1.8 convolution_add_fusion.2
  10.5 5.2 %fusion.11 = f32[256,1024]{1,0:T(8,128)} fusion(bf16[1024,1024]{1,0:T(8,128)(2,1)} %param.16, bf16[256,1024]{1,0:T(8,128)(2,1)} %bitcast.30, f32[256,1024]{1,0:T(8,128)S(1)} %convolution_add_fusion.2, bf16[256,1024]{1,0:T(8,128)(2,1)} %bitcast.26, f32[1024]{0:T(1024)S(1)} %copy-done.7), kind=kOutput, calls=%fused_computation.25 | convolution fusion | flops 1077673984 | bytes 5246976 | tf_op jit(solution)/shard_map/dot_general | solution.py:16
  15.7 3.4 fusion.1
  19.1 1.6 copy.29
  20.7 1.6 reshape.135
  22.3 18.1 %all-to-all-start = ((bf16[16,2,8192]{2,1,0:T(2,128)(2,1)}), bf16[16,2,8192]{2,1,0:T(2,128)(2,1)}, u32[]{:S(2)}, u32[]{:S(2)}) async-start(bf16[16,2,8192]{2,1,0:T(2,128)(2,1)} %reshape.135), calls=%async_computation | async-start | bytes 1048576 | tf_op jit(solution)/shard_map/all_to_all | solution.py:61
  40.6 17.3 %all-to-all-done = bf16[16,2,8192]{2,1,0:T(2,128)(2,1)} async-done(((bf16[16,2,8192]{2,1,0:T(2,128)(2,1)}), bf16[16,2,8192]{2,1,0:T(2,128)(2,1)}, u32[]{:S(2)}, u32[]{:S(2)}) %all-to-all-start) | async-done | bytes 524320 | tf_op jit(solution)/shard_map/all_to_all | solution.py:61
  57.8 2.7 reshape.136
  60.6 1.6 copy.30
  62.2 24.1 %scatter_custom_fusion.1 = f32[4096,64]{1,0:T(8,128)} fusion(s32[4096]{0:T(1024)S(1)} %bitcast.29, f32[4096,64]{1,0:T(8,128)} %bitcast.23, f32[]{:T(128)} %constant.14.clone.1), kind=kCustom, calls=%fused_computation.21 | custom fusion | flops 262144 | bytes 1049088 | tf_op jit(solution)/shard_map/scatter-add | solution.py:70
  86.3 24.1 %scatter_custom_fusion = f32[4096,64]{1,0:T(8,128)} fusion(s32[4096]{0:T(1024)S(1)} %bitcast.28, f32[4096,64]{1,0:T(8,128)} %bitcast.24, f32[]{:T(128)} %constant.14.clone.1), kind=kCustom, calls=%fused_computation.23 | custom fusion | flops 262144 | bytes 1049088 | tf_op jit(solution)/shard_map/scatter-add | solution.py:70
  110.3 3.8 add.84
  114.8 0.7 gather_fusion.2
  115.5 0.7 gather_fusion.1
  117.2 241.4 %reduce-scatter.2.cloned.1.call-done = f32[64,64]{1,0:T(8,128)} async-done(((f32[4096,64]{1,0:T(8,128)}), f32[64,64]{1,0:T(8,128)}) %reduce-scatter.2.cloned.1.call-update) | async-done | bytes 16400 | tf_op jit(solution)/shard_map/reduce_scatter | solution.py:73
  358.7 0.9 multiply_reduce_fusion
  359.6 28.5 %psum.7 = f32[64]{0:T(128)S(1)} all-reduce(f32[64]{0:T(128)S(1)} %multiply_reduce_fusion), channel_id=1, replica_groups=mesh['row'=64,'col'=16] {'col'}, use_global_device_ids=true, to_apply=%region_4.0 | all-reduce | flops 64 | bytes 512 | tf_op jit(solution)/shard_map/psum | solution.py:74
  388.1 1.3 scatter_custom_fusion.2
  389.5 0.9 copy.33
  390.4 0.8 scatter_fusion
  391.2 1.0 scatter_custom_fusion.3
  392.2 0.9 copy.34
  (28 shorter events, 1.9 us)
Async XLA Ops:
  7.2 1.6 copy-start
  7.2 3.4 copy-start.7
  19.1 21.4 %copy-start.6 = (s32[64,64,2]{1,2,0:T(2,128)S(1)}, s32[64,64,2]{1,2,0:T(2,128)}, u32[]{:S(2)}) copy-start(s32[64,64,2]{1,2,0:T(2,128)} %param.18) | copy-start | bytes 98308
  22.3 35.6 %all-to-all-start = ((bf16[16,2,8192]{2,1,0:T(2,128)(2,1)}), bf16[16,2,8192]{2,1,0:T(2,128)(2,1)}, u32[]{:S(2)}, u32[]{:S(2)}) async-start(bf16[16,2,8192]{2,1,0:T(2,128)(2,1)} %reshape.135), calls=%async_computation | async-start | bytes 1048576 | tf_op jit(solution)/shard_map/all_to_all | solution.py:61
  40.4 318.3 %reduce-scatter.2.cloned.1.call-start = ((), (), s32[]{:S(2)}) async-start(), calls=%async_computation.2 | async-start | bytes 2129920 | tf_op jit(solution)/shard_map/reduce_scatter | solution.py:73
  114.1 0.7 copy-start.8
  114.1 1.4 copy-start.2
  114.1 2.1 copy-start.4
  114.1 2.9 copy-start.5
  358.7 32.5 %copy-start.3 = (f32[64,64]{1,0:T(8,128)S(1)}, f32[64,64]{1,0:T(8,128)}, u32[]{:S(2)}) copy-start(f32[64,64]{1,0:T(8,128)} %reduce-scatter.2.cloned.1.call-done) | copy-start | bytes 49156
  391.2 1.9 copy-start.1
Sparse Core Ops, SparseCore 0:
  114.3 244.3 reduce-scatter.1
where the time goes:
time: 400 us
  waiting for transfers between devices  259 us (65%)
  other arithmetic  55.2 us (14%)
  blocking collectives  28.5 us (7%)
  starting transfers between devices  18.2 us (5%)
  local copies, waits for them, and re-layouts  14.9 us (4%)
  between operations  14.2 us (4%)
  matrix products  10.3 us (3%)
    reduce_scatter x1, waiting for transfers between devices, body(): lax.psum_scatter(all_terms, 'row', scatter_dimension=0, tiled=True)  241 us
    scatter-add x2, other arithmetic, body(): jax.ops.segment_sum(occurrences, entry_ids[:, bag_pos], num_segments=all_...  48.2 us
    psum x1, blocking collectives, body(): square_sums = lax.psum(jnp.sum(entry_grads * entry_grads, axis=1), 'col')  28.5 us
    all_to_all x1, starting transfers between devices, body(): lax.all_to_all(pooled_grad, 'col', split_axis=2, concat_axis=0, tiled=True)  18.1 us
    all_to_all x1, waiting for transfers between devices, body(): lax.all_to_all(pooled_grad, 'col', split_axis=2, concat_axis=0, tiled=True)  17.3 us
    unnamed x26, local copies, waits for them, and re-layouts  8.7 us
  transfers between devices with their start and end apart: 2, of which 2 were waited for; matrix products, arithmetic and copies ran while one was open for 1% of the time, Pallas kernels for 0%

commit v1 on v0

v1 whole, which is shorter than its diff:
```python
import functools

import jax
import jax.numpy as jnp
from jax import lax
from jax.experimental import pallas as pl
from jax.experimental.pallas import tpu as pltpu
from jax.sharding import PartitionSpec as P

MESH = pl.DeviceIdType.MESH
F32 = jnp.float32
BF16 = jnp.bfloat16

N_X = 8
N_Z = 8
N_COL = 16
FOLD = 4
SLICE = 64
BATCH = 4
BITS = 14


def peer_offset(i):
    return ((i + 1) // 2) * (2 * (i % 2) - 1)


def kernel(
    pooled, upstream, cross_w, cross_b, deep_w, deep_b, ids, touched, steps,
    grads_out, mean_square_out, stats_out,
    x_v, up_v, cw_v, dw_v,
    outgoing, incoming, codes, low_fold, onehot, acc,
    wire_out, wire_in,
    part_x, part_z, last_x, last_z,
    rows_oh, squares,
    load_sem, col_send, col_recv,
    x1_send, x1_recv, z1_send, z1_recv, x2_send, x2_recv, z2_send, z2_recv,
    sq_send, sq_recv,
):
    row, col = lax.axis_index("row"), lax.axis_index("col")
    x, z = row // N_Z, row % N_Z
    half_rows = x_v.shape[0] // 2

    def col_peer(i):
        return (col + peer_offset(i) + N_COL) % N_COL

    def x_peer(i):
        return (x + peer_offset(i) + N_X) % N_X

    def z_peer(i):
        return (z + peer_offset(i) + N_Z) % N_Z

    loads = [
        pltpu.make_async_copy(src, dst, load_sem.at[n])
        for n, (src, dst) in enumerate(
            [(pooled, x_v), (cross_w, cw_v), (deep_w, dw_v), (upstream, up_v)]
        )
    ]
    for load in loads:
        load.start()

    barrier = pltpu.get_barrier_semaphore()

    @pl.loop(1, N_COL)
    def _(i):
        pl.semaphore_signal(barrier, inc=1, device_id=(row, col_peer(i)), device_id_type=MESH)

    @pl.loop(1, N_X)
    def _(i):
        pl.semaphore_signal(
            barrier, inc=1, device_id=(x_peer(i) * N_Z + z, col), device_id_type=MESH
        )

    @pl.loop(1, N_Z)
    def _(i):
        pl.semaphore_signal(
            barrier, inc=1, device_id=(x * N_Z + z_peer(i), col), device_id_type=MESH
        )

    def col_copy(peer, slot):
        return pltpu.make_async_remote_copy(
            src_ref=outgoing.at[peer], dst_ref=incoming.at[slot],
            send_sem=col_send.at[peer], recv_sem=col_recv.at[slot],
            device_id=(row, peer), device_id_type=MESH,
        )

    fold_rows, fields = acc.shape[0], ids.shape[2]
    block = low_fold.shape[2]
    samples = ids.shape[0] // N_COL
    half_fold = fold_rows // 2
    owner_half = half_fold // (N_X * N_Z)

    def code_of(position):
        return ((128 + position % 128) << (position // 128)).astype(F32)

    codes[...] = code_of(lax.broadcasted_iota(jnp.int32, codes.shape, 0)).astype(BF16)

    def source(n):
        return col if isinstance(n, int) and n == 0 else jnp.where(
            n == 0, col, col_peer(jnp.maximum(N_COL - n, 1))
        )

    def entries_of(n):
        peer = source(n)
        pairs = [ids[peer * samples + s] for s in range(samples)]
        pieces = [pair[b:b + 1] for b in range(ids.shape[1]) for pair in pairs]
        return jnp.concatenate(pieces, axis=1)

    @pl.loop(0, N_COL)
    def _(n):
        entry = entries_of(n)
        low_fold[n] = jnp.broadcast_to((entry % FOLD).astype(F32), (16, block)).astype(BF16)
        folded = entry // FOLD
        owner_rows = 2 * owner_half
        line, owner = folded % owner_rows, folded // owner_rows
        owner_x, owner_z = owner // N_Z, owner % N_Z
        position = jnp.where(
            line < owner_half,
            (owner_x * N_Z + owner_z) * owner_half + line,
            half_fold + (owner_z * N_X + owner_x) * owner_half + line - owner_half,
        )
        wanted = jnp.broadcast_to(code_of(position), (16, block)).astype(BF16)
        one, zero = jnp.ones((), BF16), jnp.zeros((), BF16)
        row_step = 128

        @pl.loop(0, fold_rows // row_step)
        def _(k):
            at = pl.ds(k * row_step, row_step)
            here = codes[at, :].reshape(row_step // 16, 16, 128)
            for tile in range(block // 128):
                lanes_at = slice(tile * 128, (tile + 1) * 128)
                hit = jnp.where(here == wanted[None, :, lanes_at], one, zero)
                onehot[n // BATCH, at, pl.ds((n % BATCH) * block + tile * 128, 128)] = (
                    hit.reshape(row_step, 128)
                )

    low_half = lax.broadcasted_iota(jnp.int32, (half_rows, 2 * SLICE), 1) < SLICE

    loads[0].wait()
    loads[1].wait()
    scaled = jnp.dot(x_v[...], cw_v[...], preferred_element_type=F32) + cross_b[...]
    wide = x_v[...].astype(F32)
    crossed = (wide * scaled + wide).astype(BF16)
    loads[2].wait()
    hidden = jnp.dot(crossed, dw_v[...], preferred_element_type=F32) + deep_b[...]
    s = jax.nn.sigmoid(hidden)
    loads[3].wait()
    hidden_grad = (up_v[...].astype(F32) * s * (1.0 + hidden * (1.0 - s))).astype(BF16)
    crossed_grad = lax.dot_general(
        hidden_grad, dw_v[...], (((1,), (1,)), ((), ())), preferred_element_type=F32
    )
    product = (crossed_grad * wide).astype(BF16)
    back = lax.dot_general(
        product, cw_v[...], (((1,), (1,)), ((), ())), preferred_element_type=F32
    )
    grad = crossed_grad * scaled + back + crossed_grad
    for chip in range(N_COL // 2):
        tile = grad[:, chip * 2 * SLICE:(chip + 1) * 2 * SLICE]
        top, bottom = tile[:half_rows], tile[half_rows:]
        outgoing[2 * chip] = jnp.where(low_half, top, pltpu.roll(bottom, SLICE, 1)).astype(BF16)
        outgoing[2 * chip + 1] = jnp.where(
            low_half, pltpu.roll(top, SLICE, 1), bottom
        ).astype(BF16)
    pl.semaphore_wait(barrier, N_COL - 1 + N_X - 1 + N_Z - 1)

    @pl.loop(0, N_COL - 1)
    def _(n):
        col_copy(col_peer(N_COL - 1 - n), col).start()

    n_touched = touched.shape[0]
    shard_rows = grads_out.shape[1]
    lane_row = lax.broadcasted_iota(jnp.int32, (1, shard_rows), 1)
    for fold in range(FOLD):
        hits = [
            (lane_row == touched[q * FOLD + fold]).astype(F32)
            for q in range(n_touched // FOLD)
        ]
        block_oh = jnp.concatenate(hits, axis=0).astype(BF16)
        for copy in range(3):
            rows_oh[pl.ds(copy * n_touched + fold * len(hits), len(hits)), :] = block_oh
    count = (steps[...] + 1).astype(F32)
    stats_out[0:1, :] = jnp.sum(rows_oh[:n_touched, :].astype(F32), axis=0, keepdims=True)
    stats_out[1:2, :] = 1.0 - jnp.power(0.9, count)
    stats_out[2:3, :] = 1.0 - jnp.power(0.999, count)

    def spread(n):
        turned = jnp.transpose(incoming[source(n)].astype(F32)).astype(BF16)
        tokens = jnp.concatenate([turned[:SLICE], turned[SLICE:]], axis=1)
        tokens = jnp.concatenate([tokens] * (block // tokens.shape[1]), axis=1)
        tokens = tokens.reshape(SLICE // 16, 16, block)
        low = low_fold[n]
        zero = jnp.zeros((), BF16)
        return jnp.concatenate(
            [
                jnp.where((low == jnp.asarray(fold, BF16))[None], tokens, zero).reshape(SLICE, block)
                for fold in range(FOLD)
            ],
            axis=0,
        )

    incoming[col] = outgoing[col]
    acc[...] = jnp.zeros_like(acc)

    @pl.loop(0, N_COL // BATCH)
    def _(b):
        @pl.loop(b * BATCH, (b + 1) * BATCH)
        def _(n):
            @pl.when(n > 0)
            def _():
                col_copy(source(n), source(n)).wait_recv()

        tokens = jnp.concatenate([spread(b * BATCH + k) for k in range(BATCH)], axis=1)
        acc[...] += lax.dot_general(
            onehot[b], tokens, (((1,), (1,)), ((), ())), preferred_element_type=F32
        )

    chunk_rows = half_fold // N_X
    tiles = chunk_rows // 16

    def encode(axis):
        powers = []
        for half in range(2):
            piece = acc[
                axis * half_fold:(axis + 1) * half_fold, half * 128:(half + 1) * 128
            ].reshape(N_X, chunk_rows, 128)
            largest = jnp.max(jnp.abs(piece), axis=1, keepdims=True)
            power = jnp.ceil(jnp.log2(jnp.maximum(largest, 1e-30))) - BITS
            steps_of = jnp.floor(piece * jnp.exp2(-power) + 0.5).astype(jnp.int32)
            wire_out[axis, :, half * tiles:(half + 1) * tiles] = (
                steps_of.astype(jnp.int16).reshape(N_X, tiles, 16, 128)
            )
            powers.append(jnp.broadcast_to(power, (N_X, 8, 128)))
        wire_out[axis, :, 2 * tiles] = (
            jnp.concatenate(powers, axis=1).astype(jnp.int32).astype(jnp.int16)
        )

    def decode(axis, sender):
        got = wire_in[axis, sender].astype(jnp.int32).astype(F32)
        powers = jnp.exp2(got[2 * tiles])
        return jnp.concatenate(
            [
                got[half * tiles:(half + 1) * tiles].reshape(chunk_rows, 128)
                * powers[8 * half:8 * half + 1]
                for half in range(2)
            ],
            axis=1,
        )

    def to_x(src, dst, send, recv, i):
        peer = x_peer(i)
        return pltpu.make_async_remote_copy(
            src_ref=src.at[peer], dst_ref=dst.at[x],
            send_sem=send.at[peer], recv_sem=recv.at[x],
            device_id=(peer * N_Z + z, col), device_id_type=MESH,
        )

    def from_x(src, dst, send, recv, i):
        peer = x_peer(i)
        return pltpu.make_async_remote_copy(
            src_ref=src.at[peer], dst_ref=dst.at[peer],
            send_sem=send.at[peer], recv_sem=recv.at[peer],
            device_id=(peer * N_Z + z, col), device_id_type=MESH,
        )

    def to_z(src, dst, send, recv, i):
        peer = z_peer(i)
        return pltpu.make_async_remote_copy(
            src_ref=src.at[peer], dst_ref=dst.at[z],
            send_sem=send.at[peer], recv_sem=recv.at[z],
            device_id=(x * N_Z + peer, col), device_id_type=MESH,
        )

    def from_z(src, dst, send, recv, i):
        peer = z_peer(i)
        return pltpu.make_async_remote_copy(
            src_ref=src.at[peer], dst_ref=dst.at[peer],
            send_sem=send.at[peer], recv_sem=recv.at[peer],
            device_id=(x * N_Z + peer, col), device_id_type=MESH,
        )

    out_x, out_z, in_x, in_z = wire_out.at[0], wire_out.at[1], wire_in.at[0], wire_in.at[1]
    for axis in range(2):
        encode(axis)

        @pl.loop(0, N_X - 1)
        def _(n):
            if axis == 0:
                to_x(out_x, in_x, x1_send, x1_recv, N_X - 1 - n).start()
            else:
                to_z(out_z, in_z, z1_send, z1_recv, N_Z - 1 - n).start()

    part_x[...] = acc[pl.ds(x * chunk_rows, chunk_rows), :].reshape(part_x.shape)
    part_z[...] = acc[pl.ds(half_fold + z * chunk_rows, chunk_rows), :].reshape(part_z.shape)

    @pl.loop(1, N_COL)
    def _(i):
        col_copy(col_peer(i), col).wait_send()

    @pl.loop(0, N_X - 1)
    def _(n):
        from_x(out_x, in_x, x1_send, x1_recv, N_X - 1 - n).wait_recv()
        part_x[...] += decode(0, x_peer(N_X - 1 - n)).reshape(part_x.shape)

    @pl.loop(0, N_Z - 1)
    def _(n):
        to_z(part_x, last_x, z2_send, z2_recv, N_Z - 1 - n).start()

    @pl.loop(0, N_Z - 1)
    def _(n):
        from_z(out_z, in_z, z1_send, z1_recv, N_Z - 1 - n).wait_recv()
        part_z[...] += decode(1, z_peer(N_Z - 1 - n)).reshape(part_z.shape)

    @pl.loop(0, N_X - 1)
    def _(n):
        to_x(part_z, last_z, x2_send, x2_recv, N_X - 1 - n).start()

    last_x[z] = part_x[z]
    last_z[x] = part_z[x]

    @pl.loop(1, N_X)
    def _(i):
        to_x(out_x, in_x, x1_send, x1_recv, i).wait_send()
        to_z(out_z, in_z, z1_send, z1_recv, i).wait_send()

    @pl.loop(0, N_Z - 1)
    def _(n):
        from_z(part_x, last_x, z2_send, z2_recv, N_Z - 1 - n).wait_recv()
        from_x(part_z, last_z, x2_send, x2_recv, N_X - 1 - n).wait_recv()

    sum_x, sum_z = last_x[0], last_z[0]
    for n in range(1, N_X):
        sum_x, sum_z = sum_x + last_x[n], sum_z + last_z[n]

    entry = jnp.concatenate(
        [
            part[:, fold * SLICE:(fold + 1) * SLICE]
            for fold in range(FOLD) for part in (sum_x, sum_z)
        ],
        axis=0,
    )
    term_a = entry.astype(BF16)
    rest = entry - term_a.astype(F32)
    term_b = rest.astype(BF16)
    term_c = (rest - term_b.astype(F32)).astype(BF16)
    grads = lax.dot_general(
        jnp.concatenate([term_a, term_b, term_c], axis=0), rows_oh[...],
        (((0,), (0,)), ((), ())), preferred_element_type=F32,
    )

    of_rows = jnp.sum(grads * grads, axis=0, keepdims=True)
    squares[col] = jnp.concatenate(
        [of_rows[:, first:first + 128] for first in range(0, shard_rows, 128)], axis=0
    )

    def square_copy(slot, peer):
        return pltpu.make_async_remote_copy(
            src_ref=squares.at[col], dst_ref=squares.at[slot],
            send_sem=sq_send.at[peer], recv_sem=sq_recv.at[slot],
            device_id=(row, peer), device_id_type=MESH,
        )

    @pl.loop(0, N_COL - 1)
    def _(n):
        square_copy(col, col_peer(N_COL - 1 - n)).start()

    grads_out[...] = grads

    @pl.loop(1, N_X)
    def _(i):
        to_z(part_x, last_x, z2_send, z2_recv, i).wait_send()
        to_x(part_z, last_z, x2_send, x2_recv, i).wait_send()

    @pl.loop(0, N_COL - 1)
    def _(n):
        peer = col_peer(N_COL - 1 - n)
        square_copy(peer, peer).wait_recv()

    total = squares[0]
    for n in range(1, N_COL):
        total = total + squares[n]
    mean_square_out[...] = total / (SLICE * N_COL)

    @pl.loop(1, N_COL)
    def _(i):
        square_copy(col, col_peer(i)).wait_send()


def update(
    grads, mean_square, stats, table, first, second, new_table, new_first, new_second
):
    touched = stats[0:1, :] > 0.0
    second_now = 0.999 * second[...] + 0.001 * mean_square[...]
    scale = 0.01 / (stats[1:2, :] * (jnp.sqrt(second_now / stats[2:3, :]) + 1e-08))
    new_second[...] = jnp.where(touched, second_now, second[...])
    moment = 0.9 * first[...] + 0.1 * grads[...]
    new_first[...] = jnp.where(touched, moment, first[...])
    new_table[...] = jnp.where(touched, table[...] - moment * scale, table[...])


def body(
    pooled, upstream, cross_weight, cross_bias, deep_weight, deep_bias,
    bag_entries, touched_rows, table, first_moment, second_moment, step_counts,
):
    samples, fields, width = pooled.shape
    tokens = samples * fields
    hidden = upstream.shape[2]
    bags = bag_entries.shape[2]
    ids = bag_entries.transpose(0, 2, 1)
    shard_rows, columns = table.shape
    n_touched = touched_rows.shape[0]
    entries = n_touched * N_X * N_Z
    fold_rows = entries // FOLD
    owner_half = n_touched // FOLD // 2
    chunk_rows = fold_rows // 2 // N_X
    wide = FOLD * SLICE
    wire_tiles = chunk_rows // 16 * (wide // 128) + 1
    pair = 2 * SLICE
    vmem, hbm = pl.BlockSpec(memory_space=pltpu.VMEM), pl.BlockSpec(memory_space=pl.ANY)
    smem = pl.BlockSpec(memory_space=pltpu.SMEM)
    dma = pltpu.SemaphoreType.DMA
    grads, mean_square, stats = pl.pallas_call(
        kernel,
        out_shape=[
            jax.ShapeDtypeStruct((columns, shard_rows), F32),
            jax.ShapeDtypeStruct((shard_rows // 128, 128), F32),
            jax.ShapeDtypeStruct((3, shard_rows), F32),
        ],
        in_specs=[hbm, hbm, hbm, vmem, hbm, vmem, vmem, smem, vmem],
        out_specs=[vmem, vmem, vmem],
        scratch_shapes=[
            pltpu.VMEM((tokens, width), BF16),
            pltpu.VMEM((tokens, hidden), BF16),
            pltpu.VMEM((width, width), BF16),
            pltpu.VMEM((width, hidden), BF16),
            pltpu.VMEM((N_COL, tokens // 2, pair), BF16),
            pltpu.VMEM((N_COL, tokens // 2, pair), BF16),
            pltpu.VMEM((fold_rows, 128), BF16),
            pltpu.VMEM((N_COL, 16, tokens * bags), BF16),
            pltpu.VMEM((N_COL // BATCH, fold_rows, BATCH * tokens * bags), BF16),
            pltpu.VMEM((fold_rows, wide), F32),
            pltpu.VMEM((2, N_X, wire_tiles, 16, 128), jnp.int16),
            pltpu.VMEM((2, N_X, wire_tiles, 16, 128), jnp.int16),
            pltpu.VMEM((N_Z, owner_half, wide), F32),
            pltpu.VMEM((N_X, owner_half, wide), F32),
            pltpu.VMEM((N_Z, owner_half, wide), F32),
            pltpu.VMEM((N_X, owner_half, wide), F32),
            pltpu.VMEM((3 * n_touched, shard_rows), BF16),
            pltpu.VMEM((N_COL, shard_rows // 128, 128), F32),
            dma((4,)),
            dma((N_COL,)),
            dma((N_COL,)),
            dma((N_X,)), dma((N_X,)), dma((N_Z,)), dma((N_Z,)),
            dma((N_X,)), dma((N_X,)), dma((N_Z,)), dma((N_Z,)),
            dma((N_COL,)), dma((N_COL,)),
        ],
        compiler_params=pltpu.CompilerParams(
            collective_id=0, has_side_effects=True, vmem_limit_bytes=56 * 1024 * 1024
        ),
    )(
        pooled.reshape(tokens, width),
        upstream.reshape(tokens, hidden),
        cross_weight,
        cross_bias.reshape(1, width),
        deep_weight,
        deep_bias.reshape(1, hidden),
        ids,
        touched_rows,
        step_counts.reshape(1, shard_rows),
    )
    new_table, new_first, new_second = pl.pallas_call(
        update,
        out_shape=[
            jax.ShapeDtypeStruct((columns, shard_rows), F32),
            jax.ShapeDtypeStruct((columns, shard_rows), F32),
            jax.ShapeDtypeStruct((1, shard_rows), F32),
        ],
    )(
        grads,
        mean_square.reshape(1, shard_rows),
        stats,
        table.T,
        first_moment.T,
        second_moment.reshape(1, shard_rows),
    )
    return new_table.T, new_first.T, new_second.reshape(shard_rows)


def solution(mesh):
    in_specs = (
        P(("row", "col"), None, None),
        P(("row", "col"), None, None),
        P(),
        P(),
        P(),
        P(),
        P("row", None, None),
        P("row"),
        P("row", "col"),
        P("row", "col"),
        P("row"),
        P("row"),
    )
    out_specs = (P("row", "col"), P("row", "col"), P("row"))
    return jax.shard_map(body, mesh=mesh, in_specs=in_specs, out_specs=out_specs, check_vma=False)
```

time: 400 us -> 71.3 us (0.18)
  waiting for transfers between devices: 259 us -> 0 us
  Pallas kernels: 0 us -> 70.5 us
  other arithmetic: 55.2 us -> 0 us
  blocking collectives: 28.5 us -> 0 us
  starting transfers between devices: 18.2 us -> 0 us
  local copies, waits for them, and re-layouts: 14.9 us -> 0 us
  between operations: 14.2 us -> 0.64 us
  matrix products: 10.3 us -> 0 us
    reduce_scatter x1 -> x0, waiting for transfers between devices: 241 us -> none  [body(): lax.psum_scatter(all_terms, 'row', scatter_dimension=0, tiled=True)]
    pallas_call x0 -> x2, Pallas kernels: none -> 70.5 us  [the longest x1 68.5 us: body(): pl.pallas_call(kernel, out_shape=[jax.ShapeDtypeStruct((columns, shard_ro...]
    scatter-add x2 -> x0, other arithmetic: 48.2 us -> none  [body(): jax.ops.segment_sum(occurrences, entry_ids[:, bag_pos], num_segments=all_...]
    psum x1 -> x0, blocking collectives: 28.5 us -> none  [body(): square_sums = lax.psum(jnp.sum(entry_grads * entry_grads, axis=1), 'col')]
    all_to_all x1 -> x0, starting transfers between devices: 18.1 us -> none  [body(): lax.all_to_all(pooled_grad, 'col', split_axis=2, concat_axis=0, tiled=True)]
    all_to_all x1 -> x0, waiting for transfers between devices: 17.3 us -> none  [body(): lax.all_to_all(pooled_grad, 'col', split_axis=2, concat_axis=0, tiled=True)]
    dot_general x3 -> x0, matrix products: 10.3 us -> none  [the longest x1 5.16 us: cross_back(): lax.dot_general(hidden_grad, deep_weight, (((1,), (1,)), ((), ())), prefe...]
    unnamed x26 -> x0, local copies, waits for them, and re-layouts: 8.7 us -> none
  transfers between devices with their start and end apart: 2 -> 0, of which waited for: 2 -> 0; matrix products, arithmetic and copies ran while one was open for 1% -> 0% of each run, Pallas kernels for 0% -> 0%
where the time goes in v1:
time: 71.3 us; the launch traced here: 71.1 us
  Pallas kernels  70.5 us (99%)
    pallas_call x1, Pallas kernels, body(): pl.pallas_call(kernel, out_shape=[jax.ShapeDtypeStruct((columns, shard_ro...  68.5 us
    pallas_call x1, Pallas kernels, body(): pl.pallas_call(update, out_shape=[jax.ShapeDtypeStruct((columns, shard_ro...  1.98 us

profile of v1, /device:TPU:1, one launch (start us, length us, event | category | flops | bytes accessed | tf_op | source)
XLA Modules:
  0.0 71.1 jit_solution(16101578248325873952)
XLA Ops:
  0.6 68.5 %shard_map.139 = (f32[64,1024]{1,0:T(8,128)}, f32[8,128]{1,0:T(8,128)}, f32[3,1024]{1,0:T(4,128)}) custom-call(bf16[256,1024]{1,0:T(8,128)(2,1)} %bitcast.13, bf16[256,1024]{1,0:T(8,128)(2,1)} %bitcast.14, bf16[1024,1024]{1,0:T(8,128)(2,1)} %cross_w.1, f32[1,1024]{1,0:T(1,128)} %bitcast.18, bf16[1024,1024]{1,0:T(8,128)(2,1)} %deep_w.1, f32[1,1024]{1,0:T(1,128)} %bitcast.19, ...), custom_call_target="tpu_custom_call" | custom-call | tf_op jit(solution)/shard_map/pallas_call | solution.py:420
  69.2 2.0 %shard_map.140 = (f32[64,1024]{1,0:T(8,128)}, f32[64,1024]{1,0:T(8,128)}, f32[1,1024]{1,0:T(1,128)}) custom-call(f32[64,1024]{1,0:T(8,128)} %get-tuple-element.9.grads, f32[1,1024]{1,0:T(1,128)} %bitcast.22, f32[3,1024]{1,0:T(4,128)} %get-tuple-element.11.stats, f32[64,1024]{1,0:T(8,128)} %bitcast.15, f32[64,1024]{1,0:T(8,128)} %bitcast.16, f32[1,1024]{1,0:T(1,128)} %bitcast.21), custom_call_target="tpu_custom_call" | custom-call | tf_op jit(solution)/shard_map/pallas_call | solution.py:469

commit v2 on v1

--- a/solution.py
+++ b/solution.py
@@ -16,7 +16,7 @@
 N_COL = 16
 FOLD = 4
 SLICE = 64
-BATCH = 4
+BATCH = 2
 BITS = 14
 
 

time: 71.3 us -> 71.5 us (level)
  no operation moved by 1% of the time
where the time goes in v2:
time: 71.5 us; the launch traced here: 71.3 us
  Pallas kernels  70.7 us (99%)
    pallas_call x1, Pallas kernels, body(): pl.pallas_call(kernel, out_shape=[jax.ShapeDtypeStruct((columns, shard_ro...  68.7 us
    pallas_call x1, Pallas kernels, body(): pl.pallas_call(update, out_shape=[jax.ShapeDtypeStruct((columns, shard_ro...  1.98 us

profile of v2, /device:TPU:1, one launch (start us, length us, event | category | flops | bytes accessed | tf_op | source)
XLA Modules:
  0.0 71.3 jit_solution(12245337861896669054)
XLA Ops:
  0.6 68.7 %shard_map.139 = (f32[64,1024]{1,0:T(8,128)}, f32[8,128]{1,0:T(8,128)}, f32[3,1024]{1,0:T(4,128)}) custom-call(bf16[256,1024]{1,0:T(8,128)(2,1)} %bitcast.13, bf16[256,1024]{1,0:T(8,128)(2,1)} %bitcast.14, bf16[1024,1024]{1,0:T(8,128)(2,1)} %cross_w.1, f32[1,1024]{1,0:T(1,128)} %bitcast.18, bf16[1024,1024]{1,0:T(8,128)(2,1)} %deep_w.1, f32[1,1024]{1,0:T(1,128)} %bitcast.19, ...), custom_call_target="tpu_custom_call" | custom-call | tf_op jit(solution)/shard_map/pallas_call | solution.py:420
  69.3 2.0 %shard_map.140 = (f32[64,1024]{1,0:T(8,128)}, f32[64,1024]{1,0:T(8,128)}, f32[1,1024]{1,0:T(1,128)}) custom-call(f32[64,1024]{1,0:T(8,128)} %get-tuple-element.9.grads, f32[1,1024]{1,0:T(1,128)} %bitcast.22, f32[3,1024]{1,0:T(4,128)} %get-tuple-element.11.stats, f32[64,1024]{1,0:T(8,128)} %bitcast.15, f32[64,1024]{1,0:T(8,128)} %bitcast.16, f32[1,1024]{1,0:T(1,128)} %bitcast.21), custom_call_target="tpu_custom_call" | custom-call | tf_op jit(solution)/shard_map/pallas_call | solution.py:469
